TPU v7x, 512 devices: a whole 4x4x16 slice. The times are simulated.
512 devices in a mesh: group: 32 (over z, core), member: 16 (over x, y).
Axes of the slice: x: 4, y: 4, z: 16, core: 2. Of those that a mesh axis runs over, the one named last changes fastest.
Arguments:
- rhs: bfloat16 [32, 16, 768, 128], P('group', 'member'), may hold values from -6 to 6
- leaf_pivot_inverse: bfloat16 [32, 16, 768, 768], P('group', 'member'), may hold values from -1.5 to 1.5, as said below
- leaf_border_block: bfloat16 [32, 16, 512, 768], P('group', 'member'), may hold values from -0.21875 to 0.21875
- leaf_map: int32 [32, 16, 4], P('group'), may hold values from 0 to 47, as said below
- mid_inverse: bfloat16 [32, 2048, 2048], P('group', 'member'), may hold values from -1.5 to 1.5, as said below
- mid_border: bfloat16 [32, 4096, 2048], P('group', None, 'member'), may hold values from -0.125 to 0.125
- root_map: int32 [32, 16, 2], P('group', 'member'), may hold values from 0 to 3, as said below
- root_inverse: bfloat16 [8192, 8192], P('group', 'member'), may hold values from -0.5 to 0.5, as said below
Outputs:
- leaf_solution: bfloat16 [32, 16, 768, 128], P('group', 'member')
- mid_solution: bfloat16 [32, 2048, 128], P('group', 'member')
- root_solution: bfloat16 [16, 512, 128], P('member', 'group')
Inputs may be any that keep to these rules, and one draw needn't show every extreme that they name: `leaf_map`: for each (g, m) the 4 entries are distinct; a value k below 16 names pivot block k of the mid-level front, a larger one border block k - 16. `root_map`: for each (g, m) the entries are distinct. `leaf_pivot_inverse`: each [768, 768] matrix is lower triangular with a positive diagonal, as the inverse of a Cholesky factor is: every entry above the diagonal is zero. `mid_inverse`: each [2048, 2048] matrix is lower triangular with a positive diagonal, as the inverse of a Cholesky factor is: every entry above the diagonal is zero. `root_inverse`: lower triangular with a positive diagonal, as the inverse of a Cholesky factor is: every entry above the diagonal is zero.
All inputs are finite; a program needn't handle non-finite values.
Results may differ from a plain program's by a relative error of at most 0.028.
Values may be sent and summed in bfloat16 or wider, within the bound.
A program may use at most 64 MiB of HBM per device.

v0:
```python
import jax
import jax.numpy as jnp
from jax import lax
from jax.sharding import PartitionSpec as P

BLOCK = 128


def rows_for(lines, length):
    spare = -len(lines) % length
    return jnp.pad(lines, [(0, spare)] + [(0, 0)] * (lines.ndim - 1))


def sent_to_all(x, axis):
    length = lax.axis_size(axis)
    return lax.all_to_all(jnp.broadcast_to(x[None], (length, *x.shape)), axis, 0, 0, tiled=True)


def laid_out(pieces, dim):
    pieces = jnp.moveaxis(pieces, 0, dim)
    shape = pieces.shape
    return pieces.reshape(*shape[:dim], shape[dim] * shape[dim + 1], *shape[dim + 2 :])


def collect(x, axis, dim):
    pieces = sent_to_all(x, axis)
    return laid_out(pieces, dim)


def split_up(x, dim, length):
    before, after = (x.shape[:dim], x.shape[dim + 1 :])
    return jnp.moveaxis(x.reshape(*before, length, -1, *after), dim, 0)


def sum_at_owner(x, axis, dim):
    pieces = split_up(x, dim, lax.axis_size(axis))
    arrived = lax.all_to_all(pieces, axis, split_axis=0, concat_axis=0, tiled=True)
    return arrived.astype(jnp.float32).sum(axis=0)


def nested_sum(x, axes):
    lines = x.reshape(-1, x.shape[-1])
    padded = rows_for(lines, lax.axis_size(axes))
    whole = collect(sum_at_owner(padded, axes, 0).astype(jnp.bfloat16), axes, 0)
    return lax.slice_in_dim(whole, 0, len(lines)).reshape(x.shape).astype(jnp.float32)


def nested_sum_2(x, axes):
    lines = x.reshape(-1)
    own = sum_at_owner(rows_for(lines, lax.axis_size(axes)), axes, 0)
    whole = collect(own.astype(jnp.bfloat16), axes, 0)
    return whole[: len(lines)].reshape(x.shape).astype(jnp.float32)


def assemble(block_ids, targets, source_terms):
    selection_mask = (block_ids[:, None] == targets[None, :]).astype(jnp.bfloat16)
    return jnp.einsum(
        "ng,gcy->ncy", selection_mask, source_terms, preferred_element_type=jnp.float32
    )


def transposed(matrix, values):
    return lax.dot_general(
        matrix, values, (((0,), (0,)), ((), ())), preferred_element_type=jnp.float32
    )


def on_device(
    rhs,
    leaf_pivot_inverse,
    leaf_border_block,
    leaf_map,
    mid_inverse,
    mid_border,
    root_map,
    root_inverse,
):
    members = lax.axis_size("member")
    member = lax.axis_index("member")
    leaf_source = rhs[0, 0]
    leaf_cholesky_factor = leaf_pivot_inverse[0, 0]
    leaf_edge = leaf_border_block[0, 0]
    columns = leaf_source.shape[1]
    leaf_blocks = leaf_edge.shape[0] // BLOCK
    own_pivots = mid_inverse.shape[1]
    pivots = mid_inverse.shape[2]
    border_rows = mid_border.shape[1]
    pivot_blocks = pivots // BLOCK
    front_blocks = pivot_blocks + border_rows // BLOCK
    own_border = border_rows // members
    per_member = own_border // BLOCK
    group_maps = leaf_map[0]
    own_targets = lax.dynamic_index_in_dim(group_maps, member, 0, keepdims=False)
    pivot_ids = jnp.arange(pivot_blocks, dtype=jnp.int32)
    mid_factor = mid_inverse[0]
    mid_edge = mid_border[0]
    leaf_forward_solve = jnp.dot(
        leaf_cholesky_factor, leaf_source, preferred_element_type=jnp.float32
    ).astype(jnp.bfloat16)
    leaf_output = (
        -jnp.dot(leaf_edge, leaf_forward_solve, preferred_element_type=jnp.float32)
    ).astype(jnp.bfloat16)
    source_terms = leaf_output.reshape(leaf_blocks, BLOCK, columns)
    pivot_term = assemble(pivot_ids, own_targets, source_terms).reshape(pivots, columns)
    mid_rhs = nested_sum(pivot_term.astype(jnp.bfloat16), "member").astype(jnp.bfloat16)
    mid_forward = jnp.dot(mid_factor, mid_rhs, preferred_element_type=jnp.float32).astype(
        jnp.bfloat16
    )
    border_ids = pivot_blocks + jnp.arange(front_blocks - pivot_blocks, dtype=jnp.int32)
    leaf_term = assemble(border_ids, own_targets, source_terms).reshape(border_rows, columns)
    front_term = leaf_term - jnp.dot(mid_edge, mid_forward, preferred_element_type=jnp.float32)
    mid_update = sum_at_owner(front_term.astype(jnp.bfloat16), "member", 0)
    share_rows = root_inverse.shape[1]
    root_per = share_rows // BLOCK
    chooser = (root_map[0, 0][:, None] == jnp.arange(root_per, dtype=jnp.int32)[None, :]).astype(
        jnp.float32
    )
    root_term = jnp.einsum(
        "iq,ix->qx",
        chooser,
        mid_update.reshape(per_member, BLOCK * columns),
        precision=lax.Precision.HIGHEST,
    )
    root_rhs = (
        nested_sum_2(root_term.astype(jnp.bfloat16), "group")
        .reshape(share_rows, columns)
        .astype(jnp.bfloat16)
    )
    root_part = jnp.dot(root_inverse, root_rhs, preferred_element_type=jnp.float32)
    root_forward = nested_sum(root_part.astype(jnp.bfloat16), "member").astype(jnp.bfloat16)
    back_part = transposed(root_inverse, root_forward)
    root_values = nested_sum(back_part.astype(jnp.bfloat16), "group").astype(jnp.bfloat16)
    rows_out = share_rows // lax.axis_size("group")
    root_out = lax.dynamic_slice_in_dim(
        root_values, lax.axis_index("group") * rows_out, rows_out, 0
    )[None]
    own_values = jnp.einsum(
        "iq,qx->ix",
        chooser.astype(jnp.bfloat16),
        root_values.reshape(root_per, BLOCK * columns),
        preferred_element_type=jnp.float32,
    )
    own_values = own_values.astype(jnp.bfloat16).reshape(own_border, columns)
    border_values = collect(own_values, "member", 0)
    mid_back = (mid_forward.astype(jnp.float32) - transposed(mid_edge, border_values)).astype(
        jnp.bfloat16
    )
    mid_part = transposed(mid_factor, mid_back)
    mid_values = nested_sum(mid_part.astype(jnp.bfloat16), "member").astype(jnp.bfloat16)
    mid_out = lax.dynamic_slice_in_dim(mid_values, member * own_pivots, own_pivots, 0)[None]
    front_values = jnp.concatenate([mid_values, border_values], axis=0).reshape(
        front_blocks, BLOCK, columns
    )
    all_blocks = jnp.arange(front_blocks, dtype=jnp.int32)
    selected_items = (
        assemble(own_targets, all_blocks, front_values)
        .astype(jnp.bfloat16)
        .reshape(leaf_edge.shape[0], columns)
    )
    leaf_backward_solve = (
        leaf_forward_solve.astype(jnp.float32) - transposed(leaf_edge, selected_items)
    ).astype(jnp.bfloat16)
    leaf_value_rows = transposed(leaf_cholesky_factor, leaf_backward_solve).astype(jnp.bfloat16)
    return (leaf_value_rows[None, None], mid_out, root_out)


def solution(mesh):
    in_specs = (
        P("group", "member", None, None),
        P("group", "member", None, None),
        P("group", "member", None, None),
        P("group", None, None),
        P("group", "member", None),
        P("group", None, "member"),
        P("group", "member", None),
        P("group", "member"),
    )
    out_specs = (
        P("group", "member", None, None),
        P("group", "member", None),
        P("member", "group", None),
    )
    return jax.shard_map(
        on_device, mesh=mesh, in_specs=in_specs, out_specs=out_specs, check_vma=False
    )
```

profile of v0, /device:TPU:8, one launch (start us, length us, event | category | flops | bytes accessed | tf_op | source)
XLA Modules:
  0.0 235.5 jit_solution(17107032961886925404)
XLA Ops:
  0.7 1.2 copy-done
  1.9 1.4 fusion.10
  4.8 17.3 %all_to_all.66 = bf16[16,128,128]{2,1,0:T(8,128)(2,1)S(1)} all-to-all(bf16[16,128,128]{2,1,0:T(8,128)(2,1)S(1)} %copy.41), channel_id=1, replica_groups=mesh['group'=32,'member'=16] {'member'}, dimensions={0} | all-to-all | bytes 1048576 | tf_op jit(solution)/shard_map/all_to_all | solution.py:37
  22.1 0.9 broadcast_in_dim.20
  23.0 5.4 %all-to-all-start.1 = ((bf16[16,128,128]{2,1,0:T(8,128)(2,1)}), bf16[16,128,128]{2,1,0:T(8,128)(2,1)}, u32[]{:S(2)}, u32[]{:S(2)}) async-start(bf16[16,128,128]{2,1,0:T(8,128)(2,1)} %broadcast_in_dim.20), calls=%async_computation.1 | async-start | bytes 1048576 | tf_op jit(solution)/shard_map/all_to_all | solution.py:16
  28.5 0.6 fusion.44
  29.1 2.6 %copy.43 = f32[32,128,128]{2,1,0:T(8,128)} copy(f32[32,128,128]{2,0,1:T(8,128)S(1)} %fusion.44) | data formatting | bytes 4194304 | tf_op jit(solution)/shard_map/ng,gcy->ncy/dot_general | solution.py:57
  31.6 1.9 copy.44
  33.5 3.9 %all-to-all-done.1 = bf16[16,128,128]{2,1,0:T(8,128)(2,1)} async-done(((bf16[16,128,128]{2,1,0:T(8,128)(2,1)}), bf16[16,128,128]{2,1,0:T(8,128)(2,1)}, u32[]{:S(2)}, u32[]{:S(2)}) %all-to-all-start.1) | async-done | bytes 524320 | tf_op jit(solution)/shard_map/all_to_all | solution.py:16
  37.4 1.6 convolution_convert_fusion.6
  39.6 16.9 %all_to_all.67 = bf16[16,256,128]{1,2,0:T(8,128)(2,1)S(1)} all-to-all(bf16[16,256,128]{1,2,0:T(8,128)(2,1)S(1)} %bitcast.111), channel_id=1, replica_groups=mesh['group'=32,'member'=16] {'member'}, dimensions={0} | all-to-all | bytes 2097152 | tf_op jit(solution)/shard_map/all_to_all | solution.py:37
  58.1 1.4 reduce.9
  59.6 33.9 %all_to_all.68 = bf16[32,2,1024]{2,1,0:T(2,128)(2,1)S(1)} all-to-all(bf16[32,2,1024]{2,1,0:T(2,128)(2,1)S(1)} %reshape.104), channel_id=1, replica_groups=mesh['group'=32,'member'=16] {'group'}, dimensions={0} | all-to-all | bytes 262144 | tf_op jit(solution)/shard_map/all_to_all | solution.py:37
  93.9 1.4 reduce.10
  95.4 20.2 %all_to_all.69 = bf16[32,2,1024]{2,1,0:T(2,128)(2,1)S(1)} all-to-all(bf16[32,2,1024]{2,1,0:T(2,128)(2,1)S(1)} %reshape.106), channel_id=1, replica_groups=mesh['group'=32,'member'=16] {'group'}, dimensions={0} | all-to-all | bytes 262144 | tf_op jit(solution)/shard_map/all_to_all | solution.py:16
  115.7 0.7 reduce.7
  116.8 10.9 %all_to_all.70 = bf16[16,16,128]{2,1,0:T(8,128)(2,1)S(1)} all-to-all(bf16[16,16,128]{2,1,0:T(8,128)(2,1)S(1)} %bitcast.120), channel_id=1, replica_groups=mesh['group'=32,'member'=16] {'member'}, dimensions={0} | all-to-all | bytes 131072 | tf_op jit(solution)/shard_map/all_to_all | solution.py:37
  127.8 10.9 %all_to_all.71 = bf16[16,16,128]{2,1,0:T(8,128)(2,1)S(1)} all-to-all(bf16[16,16,128]{2,1,0:T(8,128)(2,1)S(1)} %broadcast_in_dim.22), channel_id=1, replica_groups=mesh['group'=32,'member'=16] {'member'}, dimensions={0} | all-to-all | bytes 131072 | tf_op jit(solution)/shard_map/all_to_all | solution.py:16
  139.0 20.2 %all_to_all.72 = bf16[32,16,128]{2,1,0:T(8,128)(2,1)S(1)} all-to-all(bf16[32,16,128]{2,1,0:T(8,128)(2,1)S(1)} %bitcast.118), channel_id=1, replica_groups=mesh['group'=32,'member'=16] {'group'}, dimensions={0} | all-to-all | bytes 262144 | tf_op jit(solution)/shard_map/all_to_all | solution.py:37
  159.2 20.2 %all_to_all.73 = bf16[32,16,128]{2,1,0:T(8,128)(2,1)S(1)} all-to-all(bf16[32,16,128]{2,1,0:T(8,128)(2,1)S(1)} %broadcast_in_dim.23), channel_id=1, replica_groups=mesh['group'=32,'member'=16] {'group'}, dimensions={0} | all-to-all | bytes 262144 | tf_op jit(solution)/shard_map/all_to_all | solution.py:16
  180.3 19.8 %all_to_all.74 = bf16[16,256,128]{2,1,0:T(8,128)(2,1)S(1)} all-to-all(bf16[16,256,128]{2,1,0:T(8,128)(2,1)S(1)} %broadcast_in_dim.25), channel_id=1, replica_groups=mesh['group'=32,'member'=16] {'member'}, dimensions={0} | all-to-all | bytes 2097152 | tf_op jit(solution)/shard_map/all_to_all | solution.py:16
  200.1 2.5 %fusion.4 = bf16[16,16,8,128]{3,2,1,0:T(8,128)(2,1)} fusion(bf16[4096,128]{1,0:T(8,128)(2,1)S(1)} %bitcast.107, bf16[1,4096,128]{2,1,0:T(8,128)(2,1)S(1)} %copy-done.2, bf16[1,128,2048]{2,1,0:T(8,128)(2,1)} %param.12, bf16[128,128]{1,0:T(8,128)(2,1)S(1)} %convolution_convert_fusion.6), kind=kOutput, calls=%fused_computation.11 | convolution fusion | flops 201637888 | bytes 3178496 | tf_op jit(solution)/shard_map/dot_general | solution.py:63
  202.6 1.2 copy.70
  203.8 13.3 %all_to_all.75 = bf16[16,128,128]{1,2,0:T(8,128)(2,1)S(1)} all-to-all(bf16[16,128,128]{1,2,0:T(8,128)(2,1)S(1)} %bitcast.115), channel_id=1, replica_groups=mesh['group'=32,'member'=16] {'member'}, dimensions={0} | all-to-all | bytes 1048576 | tf_op jit(solution)/shard_map/all_to_all | solution.py:37
  217.3 0.9 broadcast_in_dim.26
  218.2 4.8 %all-to-all-start.11 = ((bf16[16,128,128]{2,1,0:T(8,128)(2,1)}), bf16[16,128,128]{2,1,0:T(8,128)(2,1)S(1)}, u32[]{:S(2)}, u32[]{:S(2)}) async-start(bf16[16,128,128]{2,1,0:T(8,128)(2,1)} %broadcast_in_dim.26), calls=%async_computation.11 | async-start | bytes 1048576 | tf_op jit(solution)/shard_map/all_to_all | solution.py:16
  223.0 1.3 dynamic-slice_bitcast_fusion.1
  224.3 7.5 %all-to-all-done.11 = bf16[16,128,128]{2,1,0:T(8,128)(2,1)S(1)} async-done(((bf16[16,128,128]{2,1,0:T(8,128)(2,1)}), bf16[16,128,128]{2,1,0:T(8,128)(2,1)S(1)}, u32[]{:S(2)}, u32[]{:S(2)}) %all-to-all-start.11) | async-done | bytes 524320 | tf_op jit(solution)/shard_map/all_to_all | solution.py:16
  232.0 1.0 fusion.21
  233.1 0.9 fusion.18
  234.0 0.8 copy.57
  234.8 0.6 dynamic-slice_bitcast_fusion
  (56 shorter events, 6.4 us)
Async XLA Ops:
  0.6 1.3 copy-start
  0.6 2.7 %copy-start.3 = (bf16[1,1,512,768]{3,2,1,0:T(8,128)(2,1)S(1)}, bf16[1,1,512,768]{3,2,1,0:T(8,128)(2,1)}, u32[]{:S(2)}) copy-start(bf16[1,1,512,768]{3,2,1,0:T(8,128)(2,1)} %param.10) | copy-start | bytes 2359300
  1.9 2.0 copy-start.7
  23.0 14.4 %all-to-all-start.1 = ((bf16[16,128,128]{2,1,0:T(8,128)(2,1)}), bf16[16,128,128]{2,1,0:T(8,128)(2,1)}, u32[]{:S(2)}, u32[]{:S(2)}) async-start(bf16[16,128,128]{2,1,0:T(8,128)(2,1)} %broadcast_in_dim.20), calls=%async_computation.1 | async-start | bytes 1048576 | tf_op jit(solution)/shard_map/all_to_all | solution.py:16
  37.4 1.6 copy-start.1
  39.6 17.3 %copy-start.8 = (s32[1,1,2]{2,1,0:T(1,128)S(1)}, s32[1,1,2]{2,1,0:T(1,128)}, u32[]{:S(2)}) copy-start(s32[1,1,2]{2,1,0:T(1,128)} %param.14) | copy-start | bytes 28
  59.6 56.9 %copy-start.5 = (bf16[256,512]{1,0:T(8,128)(2,1)S(1)}, bf16[256,512]{1,0:T(8,128)(2,1)}, u32[]{:S(2)}) copy-start(bf16[256,512]{1,0:T(8,128)(2,1)} %param.15) | copy-start | bytes 786436
  179.4 0.7 copy-start.6
  180.1 20.0 %copy-start.2 = (bf16[1,4096,128]{2,1,0:T(8,128)(2,1)S(1)}, bf16[1,4096,128]{2,1,0:T(8,128)(2,1)}, u32[]{:S(2)}) copy-start(bf16[1,4096,128]{2,1,0:T(8,128)(2,1)} %param.13) | copy-start | bytes 3145732
  218.2 13.6 %all-to-all-start.11 = ((bf16[16,128,128]{2,1,0:T(8,128)(2,1)}), bf16[16,128,128]{2,1,0:T(8,128)(2,1)S(1)}, u32[]{:S(2)}, u32[]{:S(2)}) async-start(bf16[16,128,128]{2,1,0:T(8,128)(2,1)} %broadcast_in_dim.26), calls=%async_computation.11 | async-start | bytes 1048576 | tf_op jit(solution)/shard_map/all_to_all | solution.py:16
  232.0 1.1 copy-start.4
where the time goes:
time: 236 us; the launch traced here: 235 us
  blocking collectives  184 us (78%)
  local copies, waits for them, and re-layouts  14.6 us (6%)
  waiting for transfers between devices  11.4 us (5%)
  matrix products  10.5 us (4%)
  starting transfers between devices  10.2 us (4%)
  other arithmetic  4.19 us (2%)
    all_to_all x6, blocking collectives, sum_at_owner(): lax.all_to_all(pieces, axis, split_axis=0, concat_axis=0, tiled=True)  113 us
    all_to_all x4, blocking collectives, sent_to_all(): lax.all_to_all(jnp.broadcast_to(x[None], (length, *x.shape)), axis, 0, 0,...  71 us
    all_to_all x2, waiting for transfers between devices, sent_to_all(): lax.all_to_all(jnp.broadcast_to(x[None], (length, *x.shape)), axis, 0, 0,...  11.4 us
    all_to_all x2, starting transfers between devices, sent_to_all(): lax.all_to_all(jnp.broadcast_to(x[None], (length, *x.shape)), axis, 0, 0,...  10.2 us
  transfers between devices with their start and end apart: 2, of which 2 were waited for; matrix products, arithmetic and copies ran while one was open for 3% of the time, Pallas kernels for 0%

commit v1 on v0

v1 whole, which is shorter than its diff:
```python
import functools

import jax
import jax.numpy as jnp
from jax import lax
from jax.experimental import pallas as pl
from jax.experimental.pallas import tpu as pltpu
from jax.sharding import PartitionSpec as P

BLOCK = 128
SIDE = 4
MEMBERS = 16
CORES = 2
CHIPS = 16
GROUPS = 32
LEAF = 768
EDGE = 512
LEAF_BLOCKS = EDGE // BLOCK
PIVOTS = 2048
PIVOT_BLOCKS = PIVOTS // BLOCK
BORDER = 4096
FRONT_BLOCKS = (PIVOTS + BORDER) // BLOCK
SHARE = 512
ROOT_ROWS = 256
PIECE = 16
MESH = pl.DeviceIdType.MESH
F32 = jnp.float32
BF16 = jnp.bfloat16

MEMBER_OFFSETS = [(a, b) for a in range(SIDE) for b in range(SIDE) if a or b]
GROUP_OFFSETS = sorted(
    [(a, b) for a in range(CHIPS) for b in range(CORES) if a or b],
    key=lambda o: -min(o[0], CHIPS - o[0]),
)


def dot(a, b):
    return jnp.dot(a, b, preferred_element_type=F32)


def whole_kernel(
    rhs,
    leaf_inverse,
    leaf_edge,
    leaf_map,
    mid_inverse,
    mid_border,
    root_map,
    root_inverse,
    leaf_o,
    mid_o,
    root_o,
    v_rhs,
    v_leaf,
    v_edge,
    v_mid,
    v_border,
    v_root,
    t_leaf,
    t_edge,
    t_mid,
    t_border,
    t_root,
    forward,
    leaf_out,
    s1,
    r1,
    s2,
    r2,
    mid_forward,
    s3,
    r3,
    update,
    s4,
    r4,
    s4b,
    b_root,
    s5,
    r5,
    s5b,
    y_root,
    s6,
    r6,
    s6b,
    x_root,
    front,
    mid_back,
    s8,
    r8,
    load_sems,
    send_sems,
    m1,
    m2,
    m3,
    m5,
    m5b,
    m7,
    m8,
    m8b,
    g_sems,
):
    g = lax.axis_index("group")
    m = lax.axis_index("member")
    mx, my = m // SIDE, lax.rem(m, SIDE)
    gz, gc = g // CORES, lax.rem(g, CORES)
    members = [lax.rem(mx + a, SIDE) * SIDE + lax.rem(my + b, SIDE) for a, b in MEMBER_OFFSETS]
    groups = [lax.rem(gz + a, CHIPS) * CORES + lax.rem(gc + b, CORES) for a, b in GROUP_OFFSETS]

    barrier = pltpu.get_barrier_semaphore()
    for d in groups:
        pl.semaphore_signal(barrier, inc=1, device_id=(d, m), device_id_type=MESH)
    for d in members:
        pl.semaphore_signal(barrier, inc=1, device_id=(g, d), device_id_type=MESH)

    loads = []
    for i, (src, dst) in enumerate(
        [
            (rhs.at[0, 0], v_rhs),
            (leaf_inverse.at[0, 0], v_leaf),
            (leaf_edge.at[0, 0], v_edge),
            (mid_inverse.at[0], v_mid),
            (mid_border.at[0], v_border),
            (root_inverse, v_root),
        ]
    ):
        c = pltpu.make_async_copy(src, dst, load_sems.at[i])
        c.start()
        loads.append(c)

    def send(src, dst, ssem, rsem, device):
        c = pltpu.make_async_remote_copy(
            src_ref=src,
            dst_ref=dst,
            send_sem=ssem,
            recv_sem=rsem,
            device_id=device,
            device_id_type=MESH,
        )
        c.start()
        return c

    def drain(ref, sem):
        pltpu.make_async_copy(ref, ref, sem).wait()

    targets = [leaf_map[0, m, j] for j in range(LEAF_BLOCKS)]

    def leaf_block(k):
        idx = jnp.int32(LEAF_BLOCKS)
        for j in range(LEAF_BLOCKS):
            idx = jnp.where(targets[j] == k, j, idx)
        return leaf_out[idx]

    leaf_out[LEAF_BLOCKS] = jnp.zeros((BLOCK, BLOCK), BF16)
    loads[0].wait()
    loads[1].wait()
    for i in range(3):
        rows = pl.ds(i * 256, 256)
        depth = (i + 1) * 256
        forward[rows, :] = dot(v_leaf[rows, :depth], v_rhs[:depth, :]).astype(BF16)
    loads[2].wait()
    for j in range(LEAF_BLOCKS):
        leaf_out[j] = (-dot(v_edge[pl.ds(j * BLOCK, BLOCK), :], forward[...])).astype(BF16)

    pl.semaphore_wait(barrier, len(groups) + len(members))

    c1 = []
    for i, d in enumerate(members):
        s1[i] = leaf_block(d)
        c1.append(send(s1.at[i], r1.at[i], send_sems.at[0], m1.at[i], (g, d)))
    loads[3].wait()
    loads[4].wait()
    total = leaf_block(m).astype(F32)
    for i, c in enumerate(c1):
        c.wait_recv()
        total = total + r1[i].astype(F32)
    s2[...] = total.astype(BF16)
    c2 = []
    for i, d in enumerate(members):
        c2.append(send(s2, r2.at[m], send_sems.at[1], m2.at[i], (g, d)))
    r2[m] = s2[...]
    for c in c2:
        c.wait_recv()
    mf = dot(v_mid[...], r2[...].reshape(PIVOTS, BLOCK)).astype(BF16)
    mid_forward[...] = mf

    def border_term(d, b):
        rows = pl.ds(pl.multiple_of(d * 256 + b * BLOCK, BLOCK), BLOCK)
        return leaf_block(PIVOT_BLOCKS + 2 * d + b).astype(F32) - dot(v_border[rows, :], mid_forward[...])

    c3 = []
    for i, d in enumerate(members):
        for b in range(2):
            s3[i, b] = border_term(d, b).astype(BF16)
        c3.append(send(s3.at[i], r3.at[i], send_sems.at[2], m3.at[i], (g, d)))
    own = [border_term(m, b) for b in range(2)]
    for b in range(2):
        update[b] = own[b]
    loads[5].wait()
    for k in range(4):
        for q in range(2):
            t_root[pl.ds(k * BLOCK, BLOCK), pl.ds(q * BLOCK, BLOCK)] = v_root[
                pl.ds(q * BLOCK, BLOCK), pl.ds(k * BLOCK, BLOCK)
            ].T
    for i, c in enumerate(c3):
        c.wait_recv()
        for b in range(2):
            update[b] = update[b] + r3[i, b].astype(F32)
    update[2] = jnp.zeros((BLOCK, BLOCK), F32)

    picks = [root_map[0, 0, i] for i in range(2)]
    for q in range(4):
        idx = jnp.where(picks[0] == q, 0, jnp.where(picks[1] == q, 1, 2))
        s4[pl.ds(q * BLOCK, BLOCK), :] = update[idx].astype(BF16)

    def sum_over_groups(s, r, ssem, rsem):
        for i, d in enumerate(groups):
            rows = pl.ds(pl.multiple_of(d * PIECE, PIECE), PIECE)
            send(s.at[rows], r.at[i], ssem, rsem, (d, m))

    def finish_groups(s, r, rsem):
        drain(r, rsem)
        acc = s[pl.ds(pl.multiple_of(g * PIECE, PIECE), PIECE), :].astype(F32)
        for i in range(len(groups)):
            acc = acc + r[i].astype(F32)
        return acc.astype(BF16)

    def gather_groups(s, r, ssem, rsem):
        rows = pl.ds(pl.multiple_of(g * PIECE, PIECE), PIECE)
        for i, d in enumerate(groups):
            send(s, r.at[rows], ssem, rsem, (d, m))
        r[rows, :] = s[...]

    sum_over_groups(s4, r4, send_sems.at[3], g_sems.at[0])
    for k in range(PIVOT_BLOCKS):
        t_mid[pl.ds(k * BLOCK, BLOCK), :] = v_mid[:, pl.ds(k * BLOCK, BLOCK)].T
    s4b[...] = finish_groups(s4, r4, g_sems.at[0])
    gather_groups(s4b, b_root, send_sems.at[4], g_sems.at[1])
    for k in range(BORDER // BLOCK):
        t_border[:, pl.ds(k * BLOCK, BLOCK)] = v_border[pl.ds(k * BLOCK, BLOCK), :].T
    drain(r4, g_sems.at[1])

    s5[...] = dot(v_root[...], b_root[...]).astype(BF16)
    c5 = []
    for i, d in enumerate(members):
        rows = pl.ds(pl.multiple_of(d * PIECE, PIECE), PIECE)
        c5.append(send(s5.at[rows], r5.at[i], send_sems.at[5], m5, (g, d)))
    drain(r5, m5)
    rows = pl.ds(pl.multiple_of(m * PIECE, PIECE), PIECE)
    acc = s5[rows, :].astype(F32)
    for i in range(len(members)):
        acc = acc + r5[i].astype(F32)
    s5b[...] = acc.astype(BF16)
    for i, d in enumerate(members):
        send(s5b, y_root.at[rows], send_sems.at[6], m5b, (g, d))
    y_root[rows, :] = s5b[...]
    drain(r5, m5b)

    s6[...] = dot(t_root[...], y_root[...]).astype(BF16)
    sum_over_groups(s6, r6, send_sems.at[7], g_sems.at[2])
    for k in range(LEAF // BLOCK):
        for q in range(EDGE // BLOCK):
            t_edge[pl.ds(k * BLOCK, BLOCK), pl.ds(q * BLOCK, BLOCK)] = v_edge[
                pl.ds(q * BLOCK, BLOCK), pl.ds(k * BLOCK, BLOCK)
            ].T
    s6b[...] = finish_groups(s6, r6, g_sems.at[2])
    root_o[0] = s6b[...]
    x_rows = pl.ds(pl.multiple_of(lax.rem(g, 8) * PIECE, PIECE), PIECE)
    for i, d in enumerate(groups):
        send(s6b, x_root.at[g // 8, x_rows], send_sems.at[8], g_sems.at[3], (d, m))
    x_root[g // 8, x_rows, :] = s6b[...]
    for k in range(LEAF // BLOCK):
        for q in range(k, LEAF // BLOCK):
            t_leaf[pl.ds(k * BLOCK, BLOCK), pl.ds(q * BLOCK, BLOCK)] = v_leaf[
                pl.ds(q * BLOCK, BLOCK), pl.ds(k * BLOCK, BLOCK)
            ].T
        for q in range(k - k % 2, k):
            t_leaf[pl.ds(k * BLOCK, BLOCK), pl.ds(q * BLOCK, BLOCK)] = v_leaf[
                pl.ds(q * BLOCK, BLOCK), pl.ds(k * BLOCK, BLOCK)
            ].T
    drain(r6, g_sems.at[3])

    mine = pl.ds(PIVOT_BLOCKS + 2 * m, 2)
    for i in range(2):
        front[PIVOT_BLOCKS + 2 * m + i] = x_root[picks[i]]
    c7 = []
    for i, d in enumerate(members):
        c7.append(send(front.at[mine], front.at[mine], send_sems.at[9], m7.at[i], (g, d)))
    for c in c7:
        c.wait_recv()
    back = dot(t_border[...], front[PIVOT_BLOCKS:].reshape(BORDER, BLOCK))
    mid_back[...] = (mid_forward[...].astype(F32) - back).astype(BF16)

    def mid_term(d):
        rows = pl.ds(pl.multiple_of(d * BLOCK, BLOCK), BLOCK)
        return dot(t_mid[rows, :], mid_back[...])

    c8 = []
    for i, d in enumerate(members):
        s8[i] = mid_term(d).astype(BF16)
        c8.append(send(s8.at[i], r8.at[i], send_sems.at[10], m8.at[i], (g, d)))
    total = mid_term(m)
    for i, c in enumerate(c8):
        c.wait_recv()
        total = total + r8[i].astype(F32)
    front[m] = total.astype(BF16)
    mid_o[0] = total.astype(BF16)
    c8b = []
    for i, d in enumerate(members):
        c8b.append(send(front.at[m], front.at[m], send_sems.at[11], m8b.at[i], (g, d)))
    for c in c8b:
        c.wait_recv()

    lb = forward[...].astype(F32)
    for j in range(LEAF_BLOCKS):
        lb = lb - dot(t_edge[:, pl.ds(j * BLOCK, BLOCK)], front[targets[j]])
    lb = lb.astype(BF16)
    for i in range(3):
        leaf_o[0, 0, pl.ds(i * 256, 256), :] = dot(
            t_leaf[pl.ds(i * 256, 256), i * 256 :], lb[i * 256 :]
        ).astype(BF16)

    for i, ref in enumerate([s1, s1, s3, r4, r4, r5, r5, r4, r4, s3, s1, s1]):
        drain(ref, send_sems.at[i])


def on_device(*args):
    n_m, n_g = MEMBERS - 1, GROUPS - 1
    dma = pltpu.SemaphoreType.DMA
    block = (BLOCK, BLOCK)
    v = lambda *shape: pltpu.VMEM(shape, BF16)
    scratch = [
        v(LEAF, BLOCK),
        v(LEAF, LEAF),
        v(EDGE, LEAF),
        v(BLOCK, PIVOTS),
        v(BORDER, BLOCK),
        v(ROOT_ROWS, SHARE),
        v(LEAF, LEAF),
        v(LEAF, EDGE),
        v(PIVOTS, BLOCK),
        v(BLOCK, BORDER),
        v(SHARE, ROOT_ROWS),
        v(LEAF, BLOCK),
        v(LEAF_BLOCKS + 1, *block),
        v(n_m, *block),
        v(n_m, *block),
        v(*block),
        v(MEMBERS, *block),
        v(*block),
        v(n_m, 2, *block),
        v(n_m, 2, *block),
        pltpu.VMEM((3, *block), F32),
        v(SHARE, BLOCK),
        v(n_g, PIECE, BLOCK),
        v(PIECE, BLOCK),
        v(SHARE, BLOCK),
        v(ROOT_ROWS, BLOCK),
        v(n_m, PIECE, BLOCK),
        v(PIECE, BLOCK),
        v(ROOT_ROWS, BLOCK),
        v(SHARE, BLOCK),
        v(n_g, PIECE, BLOCK),
        v(PIECE, BLOCK),
        v(4, *block),
        v(FRONT_BLOCKS, *block),
        v(*block),
        v(n_m, *block),
        v(n_m, *block),
        dma((6,)),
        dma((12,)),
        dma((n_m,)),
        dma((n_m,)),
        dma((n_m,)),
        dma,
        dma,
        dma((n_m,)),
        dma((n_m,)),
        dma((n_m,)),
        dma((4,)),
    ]
    anywhere = pl.BlockSpec(memory_space=pl.ANY)
    scalars = pl.BlockSpec(memory_space=pltpu.SMEM)
    vmem = pl.BlockSpec(memory_space=pltpu.VMEM)
    return pl.pallas_call(
        whole_kernel,
        out_shape=(
            jax.ShapeDtypeStruct((1, 1, LEAF, BLOCK), BF16),
            jax.ShapeDtypeStruct((1, BLOCK, BLOCK), BF16),
            jax.ShapeDtypeStruct((1, PIECE, BLOCK), BF16),
        ),
        in_specs=[anywhere, anywhere, anywhere, scalars, anywhere, anywhere, scalars, anywhere],
        out_specs=(vmem, vmem, vmem),
        scratch_shapes=scratch,
        name="solve",
        compiler_params=pltpu.CompilerParams(
            collective_id=0, has_side_effects=True, vmem_limit_bytes=48 * 1024 * 1024
        ),
    )(*args)


def solution(mesh):
    in_specs = (
        P("group", "member", None, None),
        P("group", "member", None, None),
        P("group", "member", None, None),
        P("group", None, None),
        P("group", "member", None),
        P("group", None, "member"),
        P("group", "member", None),
        P("group", "member"),
    )
    out_specs = (
        P("group", "member", None, None),
        P("group", "member", None),
        P("member", "group", None),
    )
    return jax.shard_map(
        on_device, mesh=mesh, in_specs=in_specs, out_specs=out_specs, check_vma=False
    )
```

time: 236 us -> 141 us (0.60)
  the two profiles are of different devices: /device:TPU:8 before, /device:TPU:32 now
where the time goes in v1:
time: 141 us
  Pallas kernels  131 us (93%)
  local copies, waits for them, and re-layouts  9.84 us (7%)
    pallas_call x1, Pallas kernels, on_device(): pl.pallas_call(whole_kernel, out_shape=(jax.ShapeDtypeStruct((1, 1, LEAF,...  131 us
    unnamed x18, local copies, waits for them, and re-layouts  9.84 us

profile of v1, /device:TPU:32, one launch (start us, length us, event | category | flops | bytes accessed | tf_op | source)
XLA Modules:
  0.0 141.1 jit_solution(14995010699519823388)
XLA Ops:
  0.6 0.8 copy.11.leaf_map
  1.4 0.0 copy-start
  1.4 1.3 copy-done
  2.7 0.0 copy-start.1
  2.7 1.2 copy-done.1
  3.9 0.0 copy-start.2
  3.9 1.1 copy-done.2
  5.0 0.0 copy-start.3
  5.0 1.0 copy-done.3
  6.1 0.0 copy-start.4
  6.1 0.9 copy-done.4
  7.0 0.0 copy-start.5
  7.0 0.9 copy-done.5
  7.9 0.0 copy-start.6
  7.9 0.7 copy-done.6
  8.6 130.6 %solve.1 = (bf16[1,1,768,128]{3,2,1,0:T(8,128)(2,1)S(1)}, bf16[1,128,128]{2,1,0:T(8,128)(2,1)S(1)}, bf16[1,16,128]{2,1,0:T(8,128)(2,1)S(1)}) custom-call(bf16[1,1,768,128]{3,2,1,0:T(8,128)(2,1)S(1)} %copy-done.5, bf16[1,1,768,768]{3,2,1,0:T(8,128)(2,1)S(1)} %copy-done, bf16[1,1,512,768]{3,2,1,0:T(8,128)(2,1)S(1)} %copy-done.2, ...), custom_call_target="tpu_custom_call" | custom-call | tf_op jit(solution)/shard_map/solve/pallas_call | solution.py:384
  139.2 0.7 copy.15
  139.9 0.6 copy.16
  140.5 0.6 copy.17
Async XLA Ops:
  1.4 1.3 copy-start
  2.7 1.2 copy-start.1
  3.9 1.1 copy-start.2
  5.0 1.0 copy-start.3
  6.1 0.9 copy-start.4
  7.0 0.9 copy-start.5
  7.9 0.7 copy-start.6

commit v2 on v1

v2 whole, which is shorter than its diff:
```python
import functools

import jax
import jax.numpy as jnp
from jax import lax
from jax.experimental import pallas as pl
from jax.experimental.pallas import tpu as pltpu
from jax.sharding import PartitionSpec as P

BLOCK = 128
SIDE = 4
MEMBERS = 16
CORES = 2
CHIPS = 16
LEAF = 768
EDGE = 512
LEAF_BLOCKS = EDGE // BLOCK
PIVOTS = 2048
PIVOT_BLOCKS = PIVOTS // BLOCK
BORDER = 4096
FRONT_BLOCKS = (PIVOTS + BORDER) // BLOCK
SHARE = 512
ROOT_ROWS = 256
PIECE = 16
MESH = pl.DeviceIdType.MESH
F32 = jnp.float32
BF16 = jnp.bfloat16

MEMBER_OFFSETS = [
    (2, 2),
    (2, 1),
    (1, 2),
    (2, 3),
    (3, 2),
    (1, 1),
    (3, 3),
    (1, 3),
    (3, 1),
    (2, 0),
    (0, 2),
    (1, 0),
    (3, 0),
    (0, 1),
    (0, 3),
]
CHIP_OFFSETS = sorted(range(1, CHIPS), key=lambda a: -min(a, CHIPS - a))
NEAR = (2, 1, 3)


def dot(a, b):
    return jnp.dot(a, b, preferred_element_type=F32)


def whole_kernel(
    rhs,
    leaf_inverse,
    leaf_edge,
    leaf_map,
    mid_inverse,
    mid_border,
    root_map,
    root_inverse,
    leaf_o,
    mid_o,
    root_o,
    v_rhs,
    v_leaf,
    v_edge,
    v_mid,
    v_border,
    v_root,
    t_leaf,
    t_edge,
    t_mid,
    t_border,
    t_root,
    forward,
    leaf_out,
    s1,
    r1,
    s2,
    r2,
    mid_forward,
    s3,
    r3,
    line,
    u3,
    w3,
    update,
    s4,
    p4,
    u4,
    r4,
    b_root,
    s5,
    r5,
    s5b,
    y_root,
    s6,
    p6,
    u6,
    r6,
    x_root,
    x_blocks,
    front,
    mid_back,
    s8,
    r8,
    load_sems,
    send_sems,
    m1,
    t2,
    m2,
    t3,
    m3,
    t3b,
    m3b,
    m5,
    m5b,
    t7,
    m7,
    t8,
    m8,
    m8b,
    g_sems,
    pair_sems,
):
    g = lax.axis_index("group")
    m = lax.axis_index("member")
    mx, my = m // SIDE, lax.rem(m, SIDE)
    gz, gc = g // CORES, lax.rem(g, CORES)
    other = gz * CORES + 1 - gc

    def member_at(a, b):
        return lax.rem(mx + a, SIDE) * SIDE + lax.rem(my + b, SIDE)

    members, sources = [], []
    for a, b in MEMBER_OFFSETS:
        up, down = member_at(a, b), member_at((SIDE - a) % SIDE, (SIDE - b) % SIDE)
        members.append(jnp.where(gc == 0, up, down))
        sources.append(jnp.where(gc == 0, down, up))
    chips = [lax.rem(gz + a, CHIPS) for a in CHIP_OFFSETS]

    barrier = pltpu.get_barrier_semaphore()
    for z in chips:
        pl.semaphore_signal(barrier, inc=1, device_id=(z * CORES + gc, m), device_id_type=MESH)
    pl.semaphore_signal(barrier, inc=1, device_id=(other, m), device_id_type=MESH)
    for d in members:
        pl.semaphore_signal(barrier, inc=1, device_id=(g, d), device_id_type=MESH)

    loads = []
    for i, (src, dst) in enumerate(
        [
            (rhs.at[0, 0], v_rhs),
            (leaf_inverse.at[0, 0], v_leaf),
            (leaf_edge.at[0, 0], v_edge),
            (mid_inverse.at[0], v_mid),
            (mid_border.at[0], v_border),
            (root_inverse, v_root),
        ]
    ):
        c = pltpu.make_async_copy(src, dst, load_sems.at[i])
        c.start()
        loads.append(c)

    def copy_to(src, dst, ssem, rsem, device):
        return pltpu.make_async_remote_copy(
            src_ref=src,
            dst_ref=dst,
            send_sem=ssem,
            recv_sem=rsem,
            device_id=device,
            device_id_type=MESH,
        )

    def send(*args):
        c = copy_to(*args)
        c.start()
        return c

    def drain(ref, sem):
        pltpu.make_async_copy(ref, ref, sem).wait()

    sent = []
    partial_sends = []
    sent_copies = []
    pending = list(loads)

    def loaded(n):
        for _ in range(n):
            pending.pop(0).wait()

    def finish():
        loaded(len(pending))
        for ref, i in sent:
            drain(ref, i)
        for when, c in partial_sends:
            pl.when(when)(c.wait_send)
        for c in sent_copies:
            c.wait_send()

    targets = [leaf_map[0, j, m] for j in range(LEAF_BLOCKS)]

    def leaf_block(k):
        idx = jnp.int32(LEAF_BLOCKS)
        for j in range(LEAF_BLOCKS):
            idx = jnp.where(targets[j] == k, j, idx)
        return leaf_out[idx]

    leaf_out[LEAF_BLOCKS] = jnp.zeros((BLOCK, BLOCK), BF16)
    r2[...] = jnp.zeros_like(r2)
    r8[...] = jnp.zeros_like(r8)
    loaded(2)
    for i in range(3):
        rows = pl.ds(i * 256, 256)
        depth = (i + 1) * 256
        forward[rows, :] = dot(v_leaf[rows, :depth], v_rhs[:depth, :]).astype(BF16)
    loaded(1)
    for j in range(LEAF_BLOCKS):
        leaf_out[j] = (-dot(v_edge[pl.ds(j * BLOCK, BLOCK), :], forward[...])).astype(BF16)

    pl.semaphore_wait(barrier, len(chips) + 1 + len(members))

    c1 = []
    for i, d in enumerate(members):
        s1[i] = leaf_block(d)
        c1.append(send(s1.at[i], r1.at[i], send_sems.at[0], m1.at[i], (g, d)))
    loaded(2)
    sent.append((s1, send_sems.at[0]))
    total = leaf_block(m).astype(F32)
    for i, c in enumerate(c1):
        c.wait_recv()
        total = total + r1[i].astype(F32)
    s2[...] = total.astype(BF16)
    c2 = []
    for i, d in enumerate(members):
        c = copy_to(s2, r2.at[m], t2.at[i], m2.at[i], (g, d))
        pl.when(d > m)(c.start)
        partial_sends.append((d > m, c))
        c2.append(c)
    r2[m] = s2[...]
    for i, c in enumerate(c2):
        pl.when(sources[i] < m)(c.wait_recv)
    mf = dot(v_mid[...], r2[...].reshape(PIVOTS, BLOCK)).astype(BF16)
    mid_forward[...] = mf

    def border_term(d, b):
        rows = pl.ds(pl.multiple_of(d * 256 + b * BLOCK, BLOCK), BLOCK)
        return leaf_block(PIVOT_BLOCKS + 2 * d + b).astype(F32) - dot(v_border[rows, :], mid_forward[...])

    def half(a, k, h):
        return border_term(lax.rem(mx + a, SIDE) * SIDE + k if h == 0 else k * SIDE + lax.rem(my + a, SIDE), h)

    def along(a, h):
        return (g, member_at(a, 0) if h == 0 else member_at(0, a))

    c3 = []
    for a in NEAR:
        for h in range(2):
            for k in range(SIDE):
                s3[h, a - 1, k] = half(a, k, h).astype(BF16)
            c3.append(send(s3.at[h, a - 1], r3.at[h, a - 1], t3.at[h, a - 1], m3.at[h, a - 1], along(a, h)))
    for h in range(2):
        for k in range(SIDE):
            line[h, k] = half(0, k, h)
    loaded(1)
    for k in range(4):
        for q in range(2):
            t_root[pl.ds(k * BLOCK, BLOCK), pl.ds(q * BLOCK, BLOCK)] = v_root[
                pl.ds(q * BLOCK, BLOCK), pl.ds(k * BLOCK, BLOCK)
            ].T
    for c in c3:
        c.wait_recv()
    sent_copies.extend(c3)
    c3 = []
    here = (my, mx)
    for h in range(2):
        for a in NEAR:
            k = lax.rem(here[h] + a, SIDE)
            total = line[h, k]
            for q in range(3):
                total = total + r3[h, q, k].astype(F32)
            u3[h, a - 1] = total.astype(BF16)
            c3.append(
                send(u3.at[h, a - 1], w3.at[h, a - 1], t3b.at[h, a - 1], m3b.at[h, a - 1], along(a, 1 - h))
            )
    for h in range(2):
        total = line[h, here[h]]
        for q in range(3):
            total = total + r3[h, q, here[h]].astype(F32)
        update[h] = total
    for c in c3:
        c.wait_recv()
    sent_copies.extend(c3)
    for h in range(2):
        total = update[h]
        for q in range(3):
            total = total + w3[h, q].astype(F32)
        update[h] = total
    update[2] = jnp.zeros((BLOCK, BLOCK), F32)

    picks = [root_map[0, 0, i] for i in range(2)]
    for q in range(4):
        idx = jnp.where(picks[0] == q, 0, jnp.where(picks[1] == q, 1, 2))
        s4[pl.ds(q * 4, 4)] = update[idx].astype(BF16).reshape(4, CORES, PIECE, BLOCK)

    def pair_sum(s, pair, u, k):
        c = send(s.at[:, 1 - gc], pair, pair_sems.at[0, k], pair_sems.at[1, k], (other, m))
        c.wait_recv()
        sent_copies.append(c)
        u[...] = (s[:, gc].astype(F32) + pair[...].astype(F32)).astype(BF16)

    def start_sum(u, r, k):
        for i, z in enumerate(chips):
            send(u.at[z], r.at[i], g_sems.at[0, k], g_sems.at[1, k], (z * CORES + gc, m))

    def finish_sum(u, r, k):
        drain(r, g_sems.at[1, k])
        total = u[gz].astype(F32)
        for i in range(len(chips)):
            total = total + r[i].astype(F32)
        sent.append((r, g_sems.at[0, k]))
        return total.astype(BF16)

    def start_gather(r, k):
        for z in chips:
            send(r.at[gz, gc], r.at[gz, gc], g_sems.at[0, k], g_sems.at[1, k], (z * CORES + gc, m))

    def finish_gather(r, k):
        drain(r4, g_sems.at[1, k])
        sent.append((r4, g_sems.at[0, k]))
        c = send(r.at[:, gc], r.at[:, gc], pair_sems.at[0, k], pair_sems.at[1, k], (other, m))
        c.wait_recv()
        sent_copies.append(c)

    pair_sum(s4, p4, u4, 0)
    start_sum(u4, r4, 0)
    for k in range(PIVOT_BLOCKS):
        t_mid[pl.ds(k * BLOCK, BLOCK), :] = v_mid[:, pl.ds(k * BLOCK, BLOCK)].T
    b_root[gz, gc] = finish_sum(u4, r4, 0)
    start_gather(b_root, 1)
    for k in range(BORDER // BLOCK):
        t_border[:, pl.ds(k * BLOCK, BLOCK)] = v_border[pl.ds(k * BLOCK, BLOCK), :].T
    finish_gather(b_root, 1)

    s5[...] = dot(v_root[...], b_root[...].reshape(SHARE, BLOCK)).astype(BF16)
    c5 = []
    for i, d in enumerate(members):
        rows = pl.ds(pl.multiple_of(d * PIECE, PIECE), PIECE)
        c5.append(send(s5.at[rows], r5.at[i], send_sems.at[5], m5, (g, d)))
    sent.append((r5, send_sems.at[5]))
    drain(r5, m5)
    rows = pl.ds(pl.multiple_of(m * PIECE, PIECE), PIECE)
    acc = s5[rows, :].astype(F32)
    for i in range(len(members)):
        acc = acc + r5[i].astype(F32)
    s5b[...] = acc.astype(BF16)
    for i, d in enumerate(members):
        send(s5b, y_root.at[rows], send_sems.at[6], m5b, (g, d))
    y_root[rows, :] = s5b[...]
    sent.append((r5, send_sems.at[6]))
    drain(r5, m5b)

    s6[...] = dot(t_root[...], y_root[...]).astype(BF16).reshape(CHIPS, CORES, PIECE, BLOCK)
    pair_sum(s6, p6, u6, 2)
    start_sum(u6, r6, 2)
    for k in range(LEAF // BLOCK):
        for q in range(EDGE // BLOCK):
            t_edge[pl.ds(k * BLOCK, BLOCK), pl.ds(q * BLOCK, BLOCK)] = v_edge[
                pl.ds(q * BLOCK, BLOCK), pl.ds(k * BLOCK, BLOCK)
            ].T
    x_piece = finish_sum(u6, r6, 2)
    root_o[0] = x_piece
    x_root[gz, gc] = x_piece
    start_gather(x_root, 3)
    for k in range(LEAF // BLOCK):
        for q in range(k, LEAF // BLOCK):
            t_leaf[pl.ds(k * BLOCK, BLOCK), pl.ds(q * BLOCK, BLOCK)] = v_leaf[
                pl.ds(q * BLOCK, BLOCK), pl.ds(k * BLOCK, BLOCK)
            ].T
        for q in range(k - k % 2, k):
            t_leaf[pl.ds(k * BLOCK, BLOCK), pl.ds(q * BLOCK, BLOCK)] = v_leaf[
                pl.ds(q * BLOCK, BLOCK), pl.ds(k * BLOCK, BLOCK)
            ].T
    finish_gather(x_root, 3)
    x_blocks[...] = x_root[...].reshape(4, BLOCK, BLOCK)

    for h in range(2):
        front[PIVOT_BLOCKS + 2 * m + h] = x_blocks[picks[h]]

    def forward_block(a, b, h, to):
        k = PIVOT_BLOCKS + 2 * member_at((SIDE - a) % SIDE, (SIDE - b) % SIDE) + h
        a2, b2 = a + to[0], b + to[1]
        c = send(front.at[k], front.at[k], t7.at[h, a2, b2], m7.at[h, a2, b2], (g, member_at(*to)))
        sent_copies.append(c)
        return c

    c7 = {}
    for a in NEAR:
        c7[0, a, 0] = forward_block(0, 0, 0, (a, 0))
        c7[1, 0, a] = forward_block(0, 0, 1, (0, a))
    for a in NEAR:
        c7[0, 0, a] = forward_block(0, 0, 0, (0, a))
        c7[1, a, 0] = forward_block(0, 0, 1, (a, 0))
    for a in (1, 3, 2):
        c7.pop((0, a, 0)).wait_recv()
        for b in NEAR:
            c7[0, a, b] = forward_block(a, 0, 0, (0, b))
        c7.pop((1, 0, a)).wait_recv()
        for b in NEAR:
            c7[1, b, a] = forward_block(0, a, 1, (b, 0))
    for c in c7.values():
        c.wait_recv()
    back = dot(t_border[...], front[PIVOT_BLOCKS:].reshape(BORDER, BLOCK))
    mid_back[...] = (mid_forward[...].astype(F32) - back).astype(BF16)

    def mid_term(d):
        rows = pl.ds(pl.multiple_of(d * BLOCK, BLOCK), BLOCK)
        return dot(t_mid[rows, :], mid_back[...])

    c8 = []
    for i, d in enumerate(members):
        c = copy_to(s8.at[i], r8.at[i], t8.at[i], m8.at[i], (g, d))

        @pl.when(d < m)
        def _(i=i, d=d, c=c):
            s8[i] = mid_term(d).astype(BF16)
            c.start()

        partial_sends.append((d < m, c))
        c8.append(c)
    total = mid_term(m)
    for i, c in enumerate(c8):
        pl.when(sources[i] > m)(c.wait_recv)
    for i in range(len(c8)):
        total = total + r8[i].astype(F32)
    front[m] = total.astype(BF16)
    mid_o[0] = total.astype(BF16)
    c8b = []
    for i, d in enumerate(members):
        c8b.append(send(front.at[m], front.at[m], send_sems.at[11], m8b.at[i], (g, d)))
    sent.append((s1, send_sems.at[11]))
    for c in c8b:
        c.wait_recv()

    lb = forward[...].astype(F32)
    for j in range(LEAF_BLOCKS):
        lb = lb - dot(t_edge[:, pl.ds(j * BLOCK, BLOCK)], front[targets[j]])
    lb = lb.astype(BF16)
    for i in range(3):
        leaf_o[0, 0, pl.ds(i * 256, 256), :] = dot(
            t_leaf[pl.ds(i * 256, 256), i * 256 :], lb[i * 256 :]
        ).astype(BF16)

    finish()


def write_out(*refs):
    n = len(refs) // 2
    copies = [pltpu.make_async_copy(refs[i], refs[n + i], refs[-1].at[i]) for i in range(n)]
    for c in copies:
        c.start()
    for c in copies:
        c.wait()


def on_device(rhs, leaf_inverse, leaf_edge, leaf_map, *rest):
    args = (rhs, leaf_inverse, leaf_edge, jnp.swapaxes(leaf_map, 1, 2), *rest)
    n_m, n_z = MEMBERS - 1, CHIPS - 1
    piece = (PIECE, BLOCK)
    dma = pltpu.SemaphoreType.DMA
    block = (BLOCK, BLOCK)
    v = lambda *shape: pltpu.VMEM(shape, BF16)
    scratch = [
        v(LEAF, BLOCK),
        v(LEAF, LEAF),
        v(EDGE, LEAF),
        v(BLOCK, PIVOTS),
        v(BORDER, BLOCK),
        v(ROOT_ROWS, SHARE),
        v(LEAF, LEAF),
        v(LEAF, EDGE),
        v(PIVOTS, BLOCK),
        v(BLOCK, BORDER),
        v(SHARE, ROOT_ROWS),
        v(LEAF, BLOCK),
        v(LEAF_BLOCKS + 1, *block),
        v(n_m, *block),
        v(n_m, *block),
        v(*block),
        v(MEMBERS, *block),
        v(*block),
        v(2, 3, SIDE, *block),
        v(2, 3, SIDE, *block),
        pltpu.VMEM((2, SIDE, *block), F32),
        v(2, 3, *block),
        v(2, 3, *block),
        pltpu.VMEM((3, *block), F32),
        v(CHIPS, CORES, *piece),
        v(CHIPS, *piece),
        v(CHIPS, *piece),
        v(n_z, *piece),
        v(CHIPS, CORES, *piece),
        v(ROOT_ROWS, BLOCK),
        v(n_m, *piece),
        v(*piece),
        v(ROOT_ROWS, BLOCK),
        v(CHIPS, CORES, *piece),
        v(CHIPS, *piece),
        v(CHIPS, *piece),
        v(n_z, *piece),
        v(CHIPS, CORES, *piece),
        v(4, *block),
        v(FRONT_BLOCKS, *block),
        v(*block),
        v(n_m, *block),
        v(n_m, *block),
        dma((6,)),
        dma((12,)),
        dma((n_m,)),
        dma((n_m,)),
        dma((n_m,)),
        dma((2, 3)),
        dma((2, 3)),
        dma((2, 3)),
        dma((2, 3)),
        dma,
        dma,
        dma((2, SIDE, SIDE)),
        dma((2, SIDE, SIDE)),
        dma((n_m,)),
        dma((n_m,)),
        dma((n_m,)),
        dma((2, 4)),
        dma((2, 4)),
    ]
    anywhere = pl.BlockSpec(memory_space=pltpu.HBM)
    scalars = pl.BlockSpec(memory_space=pltpu.SMEM)
    vmem = pl.BlockSpec(memory_space=pltpu.VMEM)
    shapes = (
            jax.ShapeDtypeStruct((1, 1, LEAF, BLOCK), BF16),
            jax.ShapeDtypeStruct((1, BLOCK, BLOCK), BF16),
            jax.ShapeDtypeStruct((1, PIECE, BLOCK), BF16),
    )
    values = pl.pallas_call(
        whole_kernel,
        out_shape=shapes,
        in_specs=[anywhere, anywhere, anywhere, scalars, anywhere, anywhere, scalars, anywhere],
        out_specs=(vmem, vmem, vmem),
        scratch_shapes=scratch,
        name="solve",
        compiler_params=pltpu.CompilerParams(
            collective_id=0, has_side_effects=True, vmem_limit_bytes=63_000_000
        ),
    )(*args)
    return pl.pallas_call(
        write_out,
        out_shape=shapes,
        in_specs=[anywhere] * 3,
        out_specs=(anywhere,) * 3,
        scratch_shapes=[dma((3,))],
        name="write",
    )(*values)


def solution(mesh):
    in_specs = (
        P("group", "member", None, None),
        P("group", "member", None, None),
        P("group", "member", None, None),
        P("group", None, None),
        P("group", "member", None),
        P("group", None, "member"),
        P("group", "member", None),
        P("group", "member"),
    )
    out_specs = (
        P("group", "member", None, None),
        P("group", "member", None),
        P("member", "group", None),
    )
    return jax.shard_map(
        on_device, mesh=mesh, in_specs=in_specs, out_specs=out_specs, check_vma=False
    )
```

time: 141 us -> 124 us (0.88)
  the two profiles are of different devices: /device:TPU:32 before, /device:TPU:2 now
where the time goes in v2:
time: 124 us
  Pallas kernels  124 us (100%)
    pallas_call x1, Pallas kernels, on_device(): pl.pallas_call(whole_kernel, out_shape=shapes, in_specs=[anywhere, anywhe...  116 us
    pallas_call x1, Pallas kernels, on_device(): pl.pallas_call(write_out, out_shape=shapes, in_specs=[anywhere] * 3, out_...  8.2 us

profile of v2, /device:TPU:2, one launch (start us, length us, event | category | flops | bytes accessed | tf_op | source)
XLA Modules:
  0.0 124.4 jit_solution(7997147588934678580)
XLA Ops:
  0.6 115.5 %solve.1 = (bf16[1,1,768,128]{3,2,1,0:T(8,128)(2,1)}, bf16[1,128,128]{2,1,0:T(8,128)(2,1)}, bf16[1,16,128]{2,1,0:T(8,128)(2,1)}) custom-call(bf16[1,1,768,128]{3,2,1,0:T(8,128)(2,1)} %rhs.1, bf16[1,1,768,768]{3,2,1,0:T(8,128)(2,1)} %leaf_inverse.1, bf16[1,1,512,768]{3,2,1,0:T(8,128)(2,1)} %leaf_edge.1, s32[1,4,16]{2,1,0:T(4,128)} %bitcast.1, ...), custom_call_target="tpu_custom_call" | custom-call | tf_op jit(solution)/shard_map/solve/pallas_call | solution.py:545
  116.2 8.2 %write.1 = (bf16[1,1,768,128]{3,2,1,0:T(8,128)(2,1)}, bf16[1,128,128]{2,1,0:T(8,128)(2,1)}, bf16[1,16,128]{2,1,0:T(8,128)(2,1)}) custom-call(bf16[1,1,768,128]{3,2,1,0:T(8,128)(2,1)} %get-tuple-element.6.refs_0_, bf16[1,128,128]{2,1,0:T(8,128)(2,1)} %get-tuple-element.7.refs_1_, bf16[1,16,128]{2,1,0:T(8,128)(2,1)} %get-tuple-element.8.refs_2_), custom_call_target="tpu_custom_call" | custom-call | tf_op jit(solution)/shard_map/write/pallas_call | solution.py:556

commit v3 on v2

--- a/solution.py
+++ b/solution.py
@@ -44,6 +44,9 @@
     (0, 3),
 ]
 CHIP_OFFSETS = sorted(range(1, CHIPS), key=lambda a: -min(a, CHIPS - a))
+HALF_RING = CHIPS // 2
+HALF_OFFSETS = (4, 3, 13, 2, 14, 1, 15)
+SLICE = 32
 NEAR = (2, 1, 3)
 
 
@@ -140,6 +143,10 @@
         members.append(jnp.where(gc == 0, up, down))
         sources.append(jnp.where(gc == 0, down, up))
     chips = [lax.rem(gz + a, CHIPS) for a in CHIP_OFFSETS]
+    half_ring = [
+        lax.rem(gz + jnp.where(gc == 0, a, CHIPS - a), CHIPS) for a in HALF_OFFSETS
+    ]
+    gp = lax.rem(gz, HALF_RING)
 
     barrier = pltpu.get_barrier_semaphore()
     for z in chips:
@@ -244,12 +251,17 @@
     mf = dot(v_mid[...], r2[...].reshape(PIVOTS, BLOCK)).astype(BF16)
     mid_forward[...] = mf
 
-    def border_term(d, b):
-        rows = pl.ds(pl.multiple_of(d * 256 + b * BLOCK, BLOCK), BLOCK)
-        return leaf_block(PIVOT_BLOCKS + 2 * d + b).astype(F32) - dot(v_border[rows, :], mid_forward[...])
-
-    def half(a, k, h):
-        return border_term(lax.rem(mx + a, SIDE) * SIDE + k if h == 0 else k * SIDE + lax.rem(my + a, SIDE), h)
+    def terms(a, h):
+        at = lax.rem((mx, my)[h] + a, SIDE)
+        rows = v_border[at, :, h] if h == 0 else v_border[:, at, h]
+        product = dot(rows.reshape(SIDE * BLOCK, BLOCK), mid_forward[...])
+        out = []
+        for k in range(SIDE):
+            d = at * SIDE + k if h == 0 else k * SIDE + at
+            out.append(
+                leaf_block(PIVOT_BLOCKS + 2 * d + h).astype(F32) - product[k * BLOCK : (k + 1) * BLOCK]
+            )
+        return out
 
     def along(a, h):
         return (g, member_at(a, 0) if h == 0 else member_at(0, a))
@@ -257,12 +269,12 @@
     c3 = []
     for a in NEAR:
         for h in range(2):
-            for k in range(SIDE):
-                s3[h, a - 1, k] = half(a, k, h).astype(BF16)
+            for k, term in enumerate(terms(a, h)):
+                s3[h, a - 1, k] = term.astype(BF16)
             c3.append(send(s3.at[h, a - 1], r3.at[h, a - 1], t3.at[h, a - 1], m3.at[h, a - 1], along(a, h)))
     for h in range(2):
-        for k in range(SIDE):
-            line[h, k] = half(0, k, h)
+        for k, term in enumerate(terms(0, h)):
+            line[h, k] = term
     loaded(1)
     for k in range(4):
         for q in range(2):
@@ -302,7 +314,7 @@
     picks = [root_map[0, 0, i] for i in range(2)]
     for q in range(4):
         idx = jnp.where(picks[0] == q, 0, jnp.where(picks[1] == q, 1, 2))
-        s4[pl.ds(q * 4, 4)] = update[idx].astype(BF16).reshape(4, CORES, PIECE, BLOCK)
+        s4[pl.ds(q * 2, 2)] = update[idx].astype(BF16).reshape(2, CORES, SLICE, BLOCK)
 
     def pair_sum(s, pair, u, k):
         c = send(s.at[:, 1 - gc], pair, pair_sems.at[0, k], pair_sems.at[1, k], (other, m))
@@ -312,23 +324,24 @@
 
     def start_sum(u, r, k):
         for i, z in enumerate(chips):
-            send(u.at[z], r.at[i], g_sems.at[0, k], g_sems.at[1, k], (z * CORES + gc, m))
+            send(u.at[lax.rem(z, HALF_RING)], r.at[i], g_sems.at[0, k], g_sems.at[1, k], (z * CORES + gc, m))
 
     def finish_sum(u, r, k):
         drain(r, g_sems.at[1, k])
-        total = u[gz].astype(F32)
+        total = u[gp].astype(F32)
         for i in range(len(chips)):
             total = total + r[i].astype(F32)
         sent.append((r, g_sems.at[0, k]))
         return total.astype(BF16)
 
     def start_gather(r, k):
-        for z in chips:
-            send(r.at[gz, gc], r.at[gz, gc], g_sems.at[0, k], g_sems.at[1, k], (z * CORES + gc, m))
+        for z in half_ring:
+            send(r.at[gp, gc], r.at[gp, gc], g_sems.at[0, k], g_sems.at[1, k], (z * CORES + gc, m))
 
     def finish_gather(r, k):
-        drain(r4, g_sems.at[1, k])
-        sent.append((r4, g_sems.at[0, k]))
+        seven = u4.at[: len(half_ring)]
+        drain(seven, g_sems.at[1, k])
+        sent.append((seven, g_sems.at[0, k]))
         c = send(r.at[:, gc], r.at[:, gc], pair_sems.at[0, k], pair_sems.at[1, k], (other, m))
         c.wait_recv()
         sent_copies.append(c)
@@ -337,10 +350,10 @@
     start_sum(u4, r4, 0)
     for k in range(PIVOT_BLOCKS):
         t_mid[pl.ds(k * BLOCK, BLOCK), :] = v_mid[:, pl.ds(k * BLOCK, BLOCK)].T
-    b_root[gz, gc] = finish_sum(u4, r4, 0)
+    b_root[gp, gc] = finish_sum(u4, r4, 0)
     start_gather(b_root, 1)
     for k in range(BORDER // BLOCK):
-        t_border[:, pl.ds(k * BLOCK, BLOCK)] = v_border[pl.ds(k * BLOCK, BLOCK), :].T
+        t_border[:, pl.ds(k * BLOCK, BLOCK)] = v_border[k // 8, k // 2 % 4, k % 2].T
     finish_gather(b_root, 1)
 
     s5[...] = dot(v_root[...], b_root[...].reshape(SHARE, BLOCK)).astype(BF16)
@@ -361,7 +374,7 @@
     sent.append((r5, send_sems.at[6]))
     drain(r5, m5b)
 
-    s6[...] = dot(t_root[...], y_root[...]).astype(BF16).reshape(CHIPS, CORES, PIECE, BLOCK)
+    s6[...] = dot(t_root[...], y_root[...]).astype(BF16).reshape(HALF_RING, CORES, SLICE, BLOCK)
     pair_sum(s6, p6, u6, 2)
     start_sum(u6, r6, 2)
     for k in range(LEAF // BLOCK):
@@ -369,9 +382,7 @@
             t_edge[pl.ds(k * BLOCK, BLOCK), pl.ds(q * BLOCK, BLOCK)] = v_edge[
                 pl.ds(q * BLOCK, BLOCK), pl.ds(k * BLOCK, BLOCK)
             ].T
-    x_piece = finish_sum(u6, r6, 2)
-    root_o[0] = x_piece
-    x_root[gz, gc] = x_piece
+    x_root[gp, gc] = finish_sum(u6, r6, 2)
     start_gather(x_root, 3)
     for k in range(LEAF // BLOCK):
         for q in range(k, LEAF // BLOCK):
@@ -384,6 +395,8 @@
             ].T
     finish_gather(x_root, 3)
     x_blocks[...] = x_root[...].reshape(4, BLOCK, BLOCK)
+    out_rows = pl.ds(pl.multiple_of(lax.rem(g, 2) * PIECE, PIECE), PIECE)
+    root_o[0] = x_root[g // 4, lax.rem(g // 2, 2), out_rows]
 
     for h in range(2):
         front[PIVOT_BLOCKS + 2 * m + h] = x_blocks[picks[h]]
@@ -414,26 +427,25 @@
     back = dot(t_border[...], front[PIVOT_BLOCKS:].reshape(BORDER, BLOCK))
     mid_back[...] = (mid_forward[...].astype(F32) - back).astype(BF16)
 
-    def mid_term(d):
-        rows = pl.ds(pl.multiple_of(d * BLOCK, BLOCK), BLOCK)
-        return dot(t_mid[rows, :], mid_back[...])
-
     c8 = []
-    for i, d in enumerate(members):
-        c = copy_to(s8.at[i], r8.at[i], t8.at[i], m8.at[i], (g, d))
-
-        @pl.when(d < m)
-        def _(i=i, d=d, c=c):
-            s8[i] = mid_term(d).astype(BF16)
-            c.start()
-
-        partial_sends.append((d < m, c))
-        c8.append(c)
-    total = mid_term(m)
-    for i, c in enumerate(c8):
-        pl.when(sources[i] > m)(c.wait_recv)
-    for i in range(len(c8)):
-        total = total + r8[i].astype(F32)
+    for d in range(MEMBERS):
+        c8.append(copy_to(s8.at[d], r8.at[m], t8.at[d], m8.at[m], (g, d)))
+    for q in range(SIDE):
+
+        @pl.when(q <= mx)
+        def _(q=q):
+            product = dot(t_mid[pl.ds(q * SHARE, SHARE), :], mid_back[...])
+            s8[pl.ds(q * SIDE, SIDE)] = product.astype(BF16).reshape(SIDE, BLOCK, BLOCK)
+            for d in range(q * SIDE, (q + 1) * SIDE):
+                pl.when(d < m)(c8[d].start)
+
+    for d in range(MEMBERS):
+        partial_sends.append((d < m, c8[d]))
+    total = s8[m].astype(F32)
+    for d in range(MEMBERS):
+        c = copy_to(s8.at[d], r8.at[d], t8.at[d], m8.at[d], (g, d))
+        pl.when(d > m)(c.wait_recv)
+        total = total + r8[d].astype(F32)
     front[m] = total.astype(BF16)
     mid_o[0] = total.astype(BF16)
     c8b = []
@@ -456,18 +468,16 @@
 
 
 def write_out(*refs):
-    n = len(refs) // 2
-    copies = [pltpu.make_async_copy(refs[i], refs[n + i], refs[-1].at[i]) for i in range(n)]
-    for c in copies:
-        c.start()
-    for c in copies:
-        c.wait()
-
-
-def on_device(rhs, leaf_inverse, leaf_edge, leaf_map, *rest):
-    args = (rhs, leaf_inverse, leaf_edge, jnp.swapaxes(leaf_map, 1, 2), *rest)
+    for src, dst in zip(refs[:3], refs[3:]):
+        dst[...] = src[...]
+
+
+def on_device(rhs, leaf_inverse, leaf_edge, leaf_map, mid_inverse, mid_border, *rest):
+    blocks = mid_border.reshape(1, SIDE, SIDE, 2, BLOCK, BLOCK)
+    args = (rhs, leaf_inverse, leaf_edge, jnp.swapaxes(leaf_map, 1, 2), mid_inverse, blocks, *rest)
     n_m, n_z = MEMBERS - 1, CHIPS - 1
     piece = (PIECE, BLOCK)
+    part = (SLICE, BLOCK)
     dma = pltpu.SemaphoreType.DMA
     block = (BLOCK, BLOCK)
     v = lambda *shape: pltpu.VMEM(shape, BF16)
@@ -476,7 +486,7 @@
         v(LEAF, LEAF),
         v(EDGE, LEAF),
         v(BLOCK, PIVOTS),
-        v(BORDER, BLOCK),
+        v(SIDE, SIDE, 2, *block),
         v(ROOT_ROWS, SHARE),
         v(LEAF, LEAF),
         v(LEAF, EDGE),
@@ -496,25 +506,25 @@
         v(2, 3, *block),
         v(2, 3, *block),
         pltpu.VMEM((3, *block), F32),
-        v(CHIPS, CORES, *piece),
-        v(CHIPS, *piece),
-        v(CHIPS, *piece),
-        v(n_z, *piece),
-        v(CHIPS, CORES, *piece),
+        v(HALF_RING, CORES, *part),
+        v(HALF_RING, *part),
+        v(HALF_RING, *part),
+        v(n_z, *part),
+        v(HALF_RING, CORES, *part),
         v(ROOT_ROWS, BLOCK),
         v(n_m, *piece),
         v(*piece),
         v(ROOT_ROWS, BLOCK),
-        v(CHIPS, CORES, *piece),
-        v(CHIPS, *piece),
-        v(CHIPS, *piece),
-        v(n_z, *piece),
-        v(CHIPS, CORES, *piece),
+        v(HALF_RING, CORES, *part),
+        v(HALF_RING, *part),
+        v(HALF_RING, *part),
+        v(n_z, *part),
+        v(HALF_RING, CORES, *part),
         v(4, *block),
         v(FRONT_BLOCKS, *block),
         v(*block),
-        v(n_m, *block),
-        v(n_m, *block),
+        v(MEMBERS, *block),
+        v(MEMBERS, *block),
         dma((6,)),
         dma((12,)),
         dma((n_m,)),
@@ -528,8 +538,8 @@
         dma,
         dma((2, SIDE, SIDE)),
         dma((2, SIDE, SIDE)),
-        dma((n_m,)),
-        dma((n_m,)),
+        dma((MEMBERS,)),
+        dma((MEMBERS,)),
         dma((n_m,)),
         dma((2, 4)),
         dma((2, 4)),
@@ -556,9 +566,8 @@
     return pl.pallas_call(
         write_out,
         out_shape=shapes,
-        in_specs=[anywhere] * 3,
-        out_specs=(anywhere,) * 3,
-        scratch_shapes=[dma((3,))],
+        in_specs=[vmem] * 3,
+        out_specs=(vmem,) * 3,
         name="write",
     )(*values)
 

time: 124 us -> 117 us (0.944)
  Pallas kernels: 124 us -> 116 us
    pallas_call x1, Pallas kernels: 8.2 us -> 1.64 us  [on_device(): pl.pallas_call(write_out, out_shape=shapes, in_specs=[vmem] * 3, out_spec...]
where the time goes in v3:
time: 117 us
  Pallas kernels  116 us (99%)
    pallas_call x1, Pallas kernels, on_device(): pl.pallas_call(whole_kernel, out_shape=shapes, in_specs=[anywhere, anywhe...  115 us

profile of v3, /device:TPU:2, one launch (start us, length us, event | category | flops | bytes accessed | tf_op | source)
XLA Modules:
  0.0 116.8 jit_solution(2847240506147204973)
XLA Ops:
  0.6 114.5 %solve.1 = (bf16[1,1,768,128]{3,2,1,0:T(8,128)(2,1)}, bf16[1,128,128]{2,1,0:T(8,128)(2,1)}, bf16[1,16,128]{2,1,0:T(8,128)(2,1)}) custom-call(bf16[1,1,768,128]{3,2,1,0:T(8,128)(2,1)} %rhs.1, bf16[1,1,768,768]{3,2,1,0:T(8,128)(2,1)} %leaf_inverse.1, bf16[1,1,512,768]{3,2,1,0:T(8,128)(2,1)} %leaf_edge.1, s32[1,4,16]{2,1,0:T(4,128)} %bitcast.3, ...), custom_call_target="tpu_custom_call" | custom-call | tf_op jit(solution)/shard_map/solve/pallas_call | solution.py:555
  115.2 1.6 %write.1 = (bf16[1,1,768,128]{3,2,1,0:T(8,128)(2,1)}, bf16[1,128,128]{2,1,0:T(8,128)(2,1)}, bf16[1,16,128]{2,1,0:T(8,128)(2,1)}) custom-call(bf16[1,1,768,128]{3,2,1,0:T(8,128)(2,1)} %get-tuple-element.6.refs_0_, bf16[1,128,128]{2,1,0:T(8,128)(2,1)} %get-tuple-element.7.refs_1_, bf16[1,16,128]{2,1,0:T(8,128)(2,1)} %get-tuple-element.8.refs_2_), custom_call_target="tpu_custom_call" | custom-call | tf_op jit(solution)/shard_map/write/pallas_call | solution.py:566

commit v4 on v3

--- a/solution.py
+++ b/solution.py
@@ -72,11 +72,13 @@
     v_mid,
     v_border,
     v_root,
+    v_root2,
     t_leaf,
     t_edge,
     t_mid,
     t_border,
     t_root,
+    t_root2,
     forward,
     leaf_out,
     s1,
@@ -91,6 +93,7 @@
     w3,
     update,
     s4,
+    q4,
     p4,
     u4,
     r4,
@@ -99,10 +102,10 @@
     r5,
     s5b,
     y_root,
-    s6,
-    p6,
     u6,
     r6,
+    x_half,
+    x_other,
     x_root,
     x_blocks,
     front,
@@ -161,9 +164,9 @@
             (rhs.at[0, 0], v_rhs),
             (leaf_inverse.at[0, 0], v_leaf),
             (leaf_edge.at[0, 0], v_edge),
+            (root_inverse, v_root),
             (mid_inverse.at[0], v_mid),
             (mid_border.at[0], v_border),
-            (root_inverse, v_root),
         ]
     ):
         c = pltpu.make_async_copy(src, dst, load_sems.at[i])
@@ -228,6 +231,9 @@
 
     pl.semaphore_wait(barrier, len(chips) + 1 + len(members))
 
+    loaded(1)
+    c_root = send(v_root, v_root2, pair_sems.at[0, 1], pair_sems.at[1, 1], (other, m))
+    sent_copies.append(c_root)
     c1 = []
     for i, d in enumerate(members):
         s1[i] = leaf_block(d)
@@ -275,12 +281,13 @@
     for h in range(2):
         for k, term in enumerate(terms(0, h)):
             line[h, k] = term
-    loaded(1)
-    for k in range(4):
-        for q in range(2):
-            t_root[pl.ds(k * BLOCK, BLOCK), pl.ds(q * BLOCK, BLOCK)] = v_root[
-                pl.ds(q * BLOCK, BLOCK), pl.ds(k * BLOCK, BLOCK)
-            ].T
+    c_root.wait_recv()
+    for src, dst in ((v_root, t_root), (v_root2, t_root2)):
+        for k in range(4):
+            for q in range(2):
+                dst[pl.ds(k * BLOCK, BLOCK), pl.ds(q * BLOCK, BLOCK)] = src[
+                    pl.ds(q * BLOCK, BLOCK), pl.ds(k * BLOCK, BLOCK)
+                ].T
     for c in c3:
         c.wait_recv()
     sent_copies.extend(c3)
@@ -314,13 +321,33 @@
     picks = [root_map[0, 0, i] for i in range(2)]
     for q in range(4):
         idx = jnp.where(picks[0] == q, 0, jnp.where(picks[1] == q, 1, 2))
-        s4[pl.ds(q * 2, 2)] = update[idx].astype(BF16).reshape(2, CORES, SLICE, BLOCK)
-
-    def pair_sum(s, pair, u, k):
-        c = send(s.at[:, 1 - gc], pair, pair_sems.at[0, k], pair_sems.at[1, k], (other, m))
+        s4[pl.ds(q * 2, 2)] = update[idx].reshape(2, CORES, SLICE, BLOCK)
+
+    low = lax.broadcasted_iota(jnp.int32, (ROOT_ROWS, BLOCK), 1) < BLOCK // 2
+
+    def turn(x):
+        return pltpu.roll(x, BLOCK // 2, 1)
+
+    def half_of(first, second, c):
+        return jnp.where(low, jnp.where(c == 0, first, turn(first)), jnp.where(c == 0, turn(second), second))
+
+    def side_by_side(first, second):
+        return jnp.where(low, first, turn(second))
+
+    def slices(x):
+        return x.reshape(HALF_RING, SLICE, BLOCK)
+
+    def flat(x):
+        return x.reshape(ROOT_ROWS, BLOCK)
+
+    def start_pair():
+        first, second = flat(s4[:, 0]), flat(s4[:, 1])
+        q4[...] = slices(half_of(first, second, 1 - gc).astype(BF16))
+        c = send(q4, p4, pair_sems.at[0, 0], pair_sems.at[1, 0], (other, m))
+        own = half_of(first, second, gc)
         c.wait_recv()
         sent_copies.append(c)
-        u[...] = (s[:, gc].astype(F32) + pair[...].astype(F32)).astype(BF16)
+        u4[...] = slices((own + flat(p4[...]).astype(F32)).astype(BF16))
 
     def start_sum(u, r, k):
         for i, z in enumerate(chips):
@@ -336,27 +363,27 @@
 
     def start_gather(r, k):
         for z in half_ring:
-            send(r.at[gp, gc], r.at[gp, gc], g_sems.at[0, k], g_sems.at[1, k], (z * CORES + gc, m))
+            send(r.at[gp], r.at[gp], g_sems.at[0, k], g_sems.at[1, k], (z * CORES + gc, m))
 
     def finish_gather(r, k):
         seven = u4.at[: len(half_ring)]
         drain(seven, g_sems.at[1, k])
         sent.append((seven, g_sems.at[0, k]))
-        c = send(r.at[:, gc], r.at[:, gc], pair_sems.at[0, k], pair_sems.at[1, k], (other, m))
-        c.wait_recv()
-        sent_copies.append(c)
-
-    pair_sum(s4, p4, u4, 0)
+
+    start_pair()
     start_sum(u4, r4, 0)
     for k in range(PIVOT_BLOCKS):
         t_mid[pl.ds(k * BLOCK, BLOCK), :] = v_mid[:, pl.ds(k * BLOCK, BLOCK)].T
-    b_root[gp, gc] = finish_sum(u4, r4, 0)
+    b_root[gp] = finish_sum(u4, r4, 0)
     start_gather(b_root, 1)
     for k in range(BORDER // BLOCK):
         t_border[:, pl.ds(k * BLOCK, BLOCK)] = v_border[k // 8, k // 2 % 4, k % 2].T
     finish_gather(b_root, 1)
 
-    s5[...] = dot(v_root[...], b_root[...].reshape(SHARE, BLOCK)).astype(BF16)
+    b_even = flat(b_root[...]).astype(F32)
+    b_rows = jnp.concatenate([slices(b_even), slices(turn(b_even))], axis=1)
+    b_rows = b_rows.reshape(SHARE, BLOCK).astype(BF16)
+    s5[...] = side_by_side(dot(v_root[...], b_rows), dot(v_root2[...], b_rows)).astype(BF16)
     c5 = []
     for i, d in enumerate(members):
         rows = pl.ds(pl.multiple_of(d * PIECE, PIECE), PIECE)
@@ -374,16 +401,19 @@
     sent.append((r5, send_sems.at[6]))
     drain(r5, m5b)
 
-    s6[...] = dot(t_root[...], y_root[...]).astype(BF16).reshape(HALF_RING, CORES, SLICE, BLOCK)
-    pair_sum(s6, p6, u6, 2)
+    y_own = y_root[...]
+    y_other = turn(y_own.astype(F32)).astype(BF16)
+    x_part = dot(t_root[...], y_own) + dot(t_root2[...], y_other)
+    x_part = x_part.reshape(HALF_RING, CORES, SLICE, BLOCK)
+    u6[...] = slices(side_by_side(flat(x_part[:, 0]), flat(x_part[:, 1])).astype(BF16))
     start_sum(u6, r6, 2)
     for k in range(LEAF // BLOCK):
         for q in range(EDGE // BLOCK):
             t_edge[pl.ds(k * BLOCK, BLOCK), pl.ds(q * BLOCK, BLOCK)] = v_edge[
                 pl.ds(q * BLOCK, BLOCK), pl.ds(k * BLOCK, BLOCK)
             ].T
-    x_root[gp, gc] = finish_sum(u6, r6, 2)
-    start_gather(x_root, 3)
+    x_half[gp] = finish_sum(u6, r6, 2)
+    start_gather(x_half, 3)
     for k in range(LEAF // BLOCK):
         for q in range(k, LEAF // BLOCK):
             t_leaf[pl.ds(k * BLOCK, BLOCK), pl.ds(q * BLOCK, BLOCK)] = v_leaf[
@@ -393,7 +423,14 @@
             t_leaf[pl.ds(k * BLOCK, BLOCK), pl.ds(q * BLOCK, BLOCK)] = v_leaf[
                 pl.ds(q * BLOCK, BLOCK), pl.ds(k * BLOCK, BLOCK)
             ].T
-    finish_gather(x_root, 3)
+    finish_gather(x_half, 3)
+    c = send(x_half, x_other, pair_sems.at[0, 2], pair_sems.at[1, 2], (other, m))
+    c.wait_recv()
+    sent_copies.append(c)
+    mine, theirs = flat(x_half[...]).astype(F32), flat(x_other[...]).astype(F32)
+    left, right = jnp.where(gc == 0, mine, theirs), jnp.where(gc == 0, theirs, mine)
+    x_root[:, 0] = slices(jnp.where(low, left, turn(right)).astype(BF16))
+    x_root[:, 1] = slices(jnp.where(low, turn(left), right).astype(BF16))
     x_blocks[...] = x_root[...].reshape(4, BLOCK, BLOCK)
     out_rows = pl.ds(pl.multiple_of(lax.rem(g, 2) * PIECE, PIECE), PIECE)
     root_o[0] = x_root[g // 4, lax.rem(g // 2, 2), out_rows]
@@ -488,10 +525,12 @@
         v(BLOCK, PIVOTS),
         v(SIDE, SIDE, 2, *block),
         v(ROOT_ROWS, SHARE),
+        v(ROOT_ROWS, SHARE),
         v(LEAF, LEAF),
         v(LEAF, EDGE),
         v(PIVOTS, BLOCK),
         v(BLOCK, BORDER),
+        v(SHARE, ROOT_ROWS),
         v(SHARE, ROOT_ROWS),
         v(LEAF, BLOCK),
         v(LEAF_BLOCKS + 1, *block),
@@ -506,19 +545,20 @@
         v(2, 3, *block),
         v(2, 3, *block),
         pltpu.VMEM((3, *block), F32),
-        v(HALF_RING, CORES, *part),
+        pltpu.VMEM((HALF_RING, CORES, *part), F32),
+        v(HALF_RING, *part),
         v(HALF_RING, *part),
         v(HALF_RING, *part),
         v(n_z, *part),
-        v(HALF_RING, CORES, *part),
+        v(HALF_RING, *part),
         v(ROOT_ROWS, BLOCK),
         v(n_m, *piece),
         v(*piece),
         v(ROOT_ROWS, BLOCK),
-        v(HALF_RING, CORES, *part),
+        v(HALF_RING, *part),
+        v(n_z, *part),
         v(HALF_RING, *part),
         v(HALF_RING, *part),
-        v(n_z, *part),
         v(HALF_RING, CORES, *part),
         v(4, *block),
         v(FRONT_BLOCKS, *block),

time: 117 us -> 116 us (level)
    pallas_call x1, Pallas kernels: 115 us -> 113 us  [on_device(): pl.pallas_call(whole_kernel, out_shape=shapes, in_specs=[anywhere, anywhe...]
where the time goes in v4:
time: 116 us
  Pallas kernels  115 us (99%)
    pallas_call x1, Pallas kernels, on_device(): pl.pallas_call(whole_kernel, out_shape=shapes, in_specs=[anywhere, anywhe...  113 us

profile of v4, /device:TPU:2, one launch (start us, length us, event | category | flops | bytes accessed | tf_op | source)
XLA Modules:
  0.0 115.6 jit_solution(15132119407117480884)
XLA Ops:
  0.6 113.3 %solve.1 = (bf16[1,1,768,128]{3,2,1,0:T(8,128)(2,1)}, bf16[1,128,128]{2,1,0:T(8,128)(2,1)}, bf16[1,16,128]{2,1,0:T(8,128)(2,1)}) custom-call(bf16[1,1,768,128]{3,2,1,0:T(8,128)(2,1)} %rhs.1, bf16[1,1,768,768]{3,2,1,0:T(8,128)(2,1)} %leaf_inverse.1, bf16[1,1,512,768]{3,2,1,0:T(8,128)(2,1)} %leaf_edge.1, s32[1,4,16]{2,1,0:T(4,128)} %bitcast.3, ...), custom_call_target="tpu_custom_call" | custom-call | tf_op jit(solution)/shard_map/solve/pallas_call | solution.py:595
  114.0 1.6 %write.1 = (bf16[1,1,768,128]{3,2,1,0:T(8,128)(2,1)}, bf16[1,128,128]{2,1,0:T(8,128)(2,1)}, bf16[1,16,128]{2,1,0:T(8,128)(2,1)}) custom-call(bf16[1,1,768,128]{3,2,1,0:T(8,128)(2,1)} %get-tuple-element.6.refs_0_, bf16[1,128,128]{2,1,0:T(8,128)(2,1)} %get-tuple-element.7.refs_1_, bf16[1,16,128]{2,1,0:T(8,128)(2,1)} %get-tuple-element.8.refs_2_), custom_call_target="tpu_custom_call" | custom-call | tf_op jit(solution)/shard_map/write/pallas_call | solution.py:606

commit v5 on v4

--- a/solution.py
+++ b/solution.py
@@ -47,7 +47,7 @@
 HALF_RING = CHIPS // 2
 HALF_OFFSETS = (4, 3, 13, 2, 14, 1, 15)
 SLICE = 32
-NEAR = (2, 1, 3)
+NEAR = (1, 3, 2)
 
 
 def dot(a, b):
@@ -377,7 +377,7 @@
     b_root[gp] = finish_sum(u4, r4, 0)
     start_gather(b_root, 1)
     for k in range(BORDER // BLOCK):
-        t_border[:, pl.ds(k * BLOCK, BLOCK)] = v_border[k // 8, k // 2 % 4, k % 2].T
+        t_border[k // 2, :, pl.ds(k % 2 * BLOCK, BLOCK)] = v_border[k // 8, k // 2 % 4, k % 2].T
     finish_gather(b_root, 1)
 
     b_even = flat(b_root[...]).astype(F32)
@@ -459,10 +459,17 @@
         c7.pop((1, 0, a)).wait_recv()
         for b in NEAR:
             c7[1, b, a] = forward_block(0, a, 1, (b, 0))
-    for c in c7.values():
-        c.wait_recv()
-    back = dot(t_border[...], front[PIVOT_BLOCKS:].reshape(BORDER, BLOCK))
-    mid_back[...] = (mid_forward[...].astype(F32) - back).astype(BF16)
+    order = [(0, 0)] + [(a, 0) for a in NEAR] + [(0, a) for a in NEAR]
+    order += [(a, b) for a in (1, 3, 2) for b in (1, 3, 2)]
+    back = mid_forward[...].astype(F32)
+    for a, b in order:
+        for h in range(2):
+            if (h, a, b) in c7:
+                c7[h, a, b].wait_recv()
+        d = member_at((SIDE - a) % SIDE, (SIDE - b) % SIDE)
+        values = front[pl.ds(PIVOT_BLOCKS + 2 * d, 2)].reshape(2 * BLOCK, BLOCK)
+        back = back - dot(t_border[d], values)
+    mid_back[...] = back.astype(BF16)
 
     c8 = []
     for d in range(MEMBERS):
@@ -529,7 +536,7 @@
         v(LEAF, LEAF),
         v(LEAF, EDGE),
         v(PIVOTS, BLOCK),
-        v(BLOCK, BORDER),
+        v(MEMBERS, BLOCK, 2 * BLOCK),
         v(SHARE, ROOT_ROWS),
         v(SHARE, ROOT_ROWS),
         v(LEAF, BLOCK),

time: 116 us -> 116 us (level)
  no operation moved by 1% of the time
where the time goes in v5:
time: 116 us
  Pallas kernels  116 us (100%)
    pallas_call x1, Pallas kernels, on_device(): pl.pallas_call(whole_kernel, out_shape=shapes, in_specs=[anywhere, anywhe...  114 us

profile of v5, /device:TPU:2, one launch (start us, length us, event | category | flops | bytes accessed | tf_op | source)
XLA Modules:
  0.0 116.3 jit_solution(6697102718617179734)
XLA Ops:
  0.6 114.0 %solve.1 = (bf16[1,1,768,128]{3,2,1,0:T(8,128)(2,1)}, bf16[1,128,128]{2,1,0:T(8,128)(2,1)}, bf16[1,16,128]{2,1,0:T(8,128)(2,1)}) custom-call(bf16[1,1,768,128]{3,2,1,0:T(8,128)(2,1)} %rhs.1, bf16[1,1,768,768]{3,2,1,0:T(8,128)(2,1)} %leaf_inverse.1, bf16[1,1,512,768]{3,2,1,0:T(8,128)(2,1)} %leaf_edge.1, s32[1,4,16]{2,1,0:T(4,128)} %bitcast.3, ...), custom_call_target="tpu_custom_call" | custom-call | tf_op jit(solution)/shard_map/solve/pallas_call | solution.py:602
  114.6 1.6 %write.1 = (bf16[1,1,768,128]{3,2,1,0:T(8,128)(2,1)}, bf16[1,128,128]{2,1,0:T(8,128)(2,1)}, bf16[1,16,128]{2,1,0:T(8,128)(2,1)}) custom-call(bf16[1,1,768,128]{3,2,1,0:T(8,128)(2,1)} %get-tuple-element.6.refs_0_, bf16[1,128,128]{2,1,0:T(8,128)(2,1)} %get-tuple-element.7.refs_1_, bf16[1,16,128]{2,1,0:T(8,128)(2,1)} %get-tuple-element.8.refs_2_), custom_call_target="tpu_custom_call" | custom-call | tf_op jit(solution)/shard_map/write/pallas_call | solution.py:613
